TPU v7x, 32 devices: a whole 2x2x4 slice. The times are simulated.
32 devices in a mesh: phi: 8 (over z, core), mom: 4 (over y, x).
Axes of the slice: x: 2, y: 2, z: 4, core: 2. Of those that a mesh axis runs over, the one named last changes fastest.
Arguments:
- spectra: float32 [32, 4, 16, 64, 256], P('mom', None, 'phi'), may hold values from 0.1 to 3
- production: bfloat16 [32, 32], replicated, may hold values from 0 to 0.119628906
- bin_group: int32 [32], replicated, may hold values from 0 to 3
- parent_of: int32 [4], replicated, may hold values from 0 to 3
- diffusivity: float32 [64, 256], replicated, may hold values from 0.05 to 0.22
- height_inverse: float32 [64, 64], replicated, may hold values from -1 to 1, as said below
- loss_rate: float32 [32], P('mom'), may hold values from 2 to 20
- density: float32 [16, 64, 256], P('phi'), may hold values from 0.5 to 2
Outputs:
- spectra_out: float32 [32, 4, 16, 64, 256], P('mom', None, 'phi')
Inputs may be any that keep to these rules, and one draw needn't show every extreme that they name: `height_inverse`: diagonal entries lie between 0.7 and 1, off-diagonal entries are small.
All inputs are finite; a program needn't handle non-finite values.
Results may differ from a plain program's by a relative error of at most 0.00085.
Values may be sent and summed in bfloat16 or wider, within the bound.
A program may use at most 64 MiB of HBM per device.

v0:
```python
import jax
import jax.numpy as jnp
from jax import lax
from jax.sharding import PartitionSpec as P


def padded_2(cells, sides, width):
    for axis, dim in sides:
        count = lax.axis_size(axis)
        head = lax.slice_in_dim(cells, 0, width, axis=dim)
        tail = lax.slice_in_dim(cells, cells.shape[dim] - width, cells.shape[dim], axis=dim)
        cells = jnp.concatenate(
            [
                lax.ppermute(tail, axis, [(i, (i + 1) % count) for i in range(count)]),
                cells,
                lax.ppermute(head, axis, [((i + 1) % count, i) for i in range(count)]),
            ],
            axis=dim,
        )
    return cells


def passed_along(block, axis, distance):
    devices = range(lax.axis_size(axis))
    route = [(i - distance, i) for i in devices if i - distance in devices]
    return lax.ppermute(block, axis, route)


def one_step(
    state, production, bin_group, parent_of, diffusivity, height_inverse, loss_rate, density
):
    bins_here = state.shape[0]
    species = state.shape[1]
    onehot = (parent_of[:, None] == jnp.arange(species, dtype=jnp.int32)[None, :]).astype(
        jnp.float32
    )
    parents = jnp.einsum("st,qtxzr->qsxzr", onehot, state, precision=lax.Precision.HIGHEST).astype(
        jnp.bfloat16
    )
    same = bin_group[:, None] == bin_group[None, :]
    kernel = jnp.where(same, production, jnp.zeros_like(production))
    first_bin = lax.axis_index("mom") * bins_here
    flat_parents = parents.reshape(bins_here, -1)
    kernel_rows = lax.dynamic_slice_in_dim(kernel, first_bin, bins_here, 0)
    source = jnp.dot(
        kernel_rows,
        lax.all_gather(flat_parents, "mom", axis=0, tiled=True),
        preferred_element_type=jnp.float32,
    )
    sourced = state + source.reshape(state.shape)
    padded = padded_2(sourced.astype(jnp.bfloat16), (("phi", 2),), 1).astype(sourced.dtype)
    lap_phi = padded[:, :, 2:] + padded[:, :, :-2] - 2.0 * sourced
    pad_r = jnp.pad(sourced, ((0, 0), (0, 0), (0, 0), (0, 0), (1, 1)))
    lap_r = pad_r[..., 2:] + pad_r[..., :-2] - 2.0 * sourced
    moved = sourced + diffusivity * lap_phi + 0.5 * diffusivity * lap_r
    pad_z = jnp.pad(moved, ((0, 0), (0, 0), (0, 0), (1, 1), (0, 0)))
    halfway = moved + 0.25 * (pad_z[:, :, :, 2:] + pad_z[:, :, :, :-2] - 2.0 * moved)
    settled = jnp.einsum(
        "yz,psxzr->psxyr", height_inverse, halfway, precision=lax.Precision.HIGHEST
    )
    loss_coef = loss_rate[:, None, None, None, None] * density[None, None]
    upper_settled, upper_rate = passed_along((settled[:1], loss_rate[:1]), "mom", -1)
    upper_coef = upper_rate[:, None, None, None, None] * density[None, None]
    coef_next = jnp.concatenate([loss_coef[1:], upper_coef], axis=0)
    settled_next = jnp.concatenate([settled[1:], upper_settled], axis=0)
    right_side = (1.0 - 0.5 * loss_coef) * settled + 0.5 * coef_next * settled_next
    denominator = 1.0 + 0.5 * loss_coef
    offsets = right_side / denominator
    factors = 0.5 * coef_next / denominator
    local_c = jnp.zeros(state.shape[1:], jnp.float32)
    local_g = jnp.ones(factors.shape[1:], jnp.float32)
    for level in range(bins_here - 1, -1, -1):
        local_c = offsets[level] + factors[level] * local_c
        local_g = factors[level] * local_g

    def relay_step(index, incoming):
        return passed_along(local_c + local_g * incoming, "mom", -1)

    incoming = lax.fori_loop(0, lax.axis_size("mom") - 1, relay_step, jnp.zeros_like(local_c))
    current = incoming
    levels = []
    for level in range(bins_here - 1, -1, -1):
        current = offsets[level] + factors[level] * current
        levels.append(current)
    return jnp.stack(levels[::-1], axis=0)


def local(
    spectra, production, bin_group, parent_of, diffusivity, height_inverse, loss_rate, density
):
    state = spectra
    state = one_step(
        state, production, bin_group, parent_of, diffusivity, height_inverse, loss_rate, density
    )
    return state


def solution(mesh):
    return jax.shard_map(
        local,
        mesh=mesh,
        in_specs=(
            P("mom", None, "phi", None, None),
            P(),
            P(),
            P(),
            P(),
            P(),
            P("mom"),
            P("phi", None, None),
        ),
        out_specs=P("mom", None, "phi", None, None),
        check_vma=False,
    )
```

profile of v0, /device:TPU:0, one launch (start us, length us, event | category | flops | bytes accessed | tf_op | source)
XLA Modules:
  0.0 232.6 jit_solution(12985421989858237578)
XLA Ops:
  6.5 8.7 %convert_bitcast_fusion = bf16[8,4,2,64,256]{4,1,3,2,0:T(4,128)(2,1)S(1)} fusion(f32[8,4,2,64,256]{4,3,2,1,0:T(8,128)} %param.10, s32[4]{0:T(128)} %param.13), kind=kOutput, calls=%fused_computation.29 | convolution fusion | flops 51380240 | bytes 6291472 | tf_op jit(solution)/shard_map/st,qtxzr->qsxzr/dot_general | solution.py:37
  15.3 0.4 copy.12
  15.7 0.0 copy-start.8
  15.7 0.0 copy-start.4
  15.7 2.5 %copy.16 = bf16[1,8,512,256]{3,1,2,0:T(8,128)(2,1)} copy(bf16[1,8,512,256]{3,2,1,0:T(8,128)(2,1)S(1)} %bitcast.138) | data formatting | bytes 4194304
  18.2 0.0 all-gather.2.cloned.1.call-update
  18.2 1.3 collective-permute-start.3
  19.6 0.1 dynamic-slice
  19.6 0.2 broadcast_multiply_fusion
  19.8 88.9 %all-gather.2.cloned.1.call-done = bf16[32,131072]{1,0:T(8,128)(2,1)} async-done(((bf16[8,131072]{1,0:T(8,128)(2,1)}), bf16[32,131072]{1,0:T(8,128)(2,1)}) %all-gather.2.cloned.1.call-update) | async-done | bytes 8388624 | tf_op jit(solution)/shard_map/all_gather | solution.py:47
  108.7 4.8 %fusion.29 = f32[8,131072]{1,0:T(8,128)S(1)} fusion(bf16[32,131072]{1,0:T(8,128)(2,1)} %all-gather.2.cloned.1.call-done, bf16[32,32]{1,0:T(8,128)(2,1)} %param.11, s32[]{:T(128)S(6)} %select_n.8, s32[32]{0:T(128)S(1)} %copy-done.8, s32[8]{0:T(128)S(1)} %dynamic-slice), kind=kOutput, calls=%fused_computation.76 | convolution fusion | flops 67109376 | bytes 12585124 | tf_op jit(solution)/shard_map/dot_general | solution.py:45
  113.5 1.6 fusion.42
  115.2 0.2 fusion.43
  115.4 0.2 collective-permute-start.1
  115.7 3.5 %collective-permute-start.2 = (bf16[8,4,1,64,256]{4,3,2,1,0:T(8,128)(2,1)S(1)}, bf16[8,4,1,64,256]{4,3,2,1,0:T(8,128)(2,1)S(1)}, u32[]{:S(2)}, u32[]{:S(2)}) collective-permute-start(bf16[8,4,1,64,256]{4,3,2,1,0:T(8,128)(2,1)S(1)} %get-tuple-element.43), channel_id=1, source_target_pairs={{4,0},{8,4},{12,8},{16,12},{20,16},{24,20},{28,24},{0,28},{5,1},{9... | collective-permute-start | bytes 3145736 | tf_op jit(solution)/shard_map/ppermute | solution.py:16
  119.2 0.2 fusion.44
  119.4 0.3 fusion.27
  119.7 0.6 multiply_bitcast_fusion.1
  120.4 0.3 fusion.25
  120.7 20.4 %collective-permute-done.1 = bf16[8,4,1,64,256]{4,3,2,1,0:T(8,128)(2,1)S(1)} collective-permute-done((bf16[8,4,1,64,256]{4,3,2,1,0:T(8,128)(2,1)S(1)}, bf16[8,4,1,64,256]{4,3,2,1,0:T(8,128)(2,1)S(1)}, u32[]{:S(2)}, u32[]{:S(2)}) %collective-permute-start.1) | collective-permute-done | bytes 1048608 | tf_op jit(solution)/shard_map/ppermute | solution.py:14
  141.0 0.6 maximum_convert_fusion
  141.7 2.9 %fusion.9 = f32[8,4,2,64,256]{4,3,2,1,0:T(8,128)S(1)} fusion(f32[8,4,2,64,256]{4,3,2,1,0:T(8,128)S(1)} %get-tuple-element.41, f32[8,4,4,64,256]{4,3,2,1,0:T(8,128)S(1)} %maximum_convert_fusion, f32[64,256]{1,0:T(8,128)S(1)} %broadcast_multiply_fusion.2, f32[64,256]{1,0:T(8,128)S(1)} %copy-done.5), kind=kLoop, calls=%fused_computation.13 | loop fusion | flops 9437184 | bytes 16908288 | tf_op jit(solution)/shard_map/add | solution.py:55
  144.6 5.4 %fusion.18 = f32[8,4,2,64,256]{4,3,2,1,0:T(8,128)S(1)} fusion(f32[8,4,2,64,256]{4,3,2,1,0:T(8,128)S(1)} %fusion.9, f32[64,64]{1,0:T(8,128)S(1)} %copy-done), kind=kOutput, calls=%fused_computation.26 | convolution fusion | flops 810549248 | bytes 8404992 | tf_op jit(solution)/shard_map/yz,psxzr->psxyr/dot_general | solution.py:58
  150.0 1.3 collective-permute-start.4
  151.3 0.1 maximum_multiply_fusion.1
  151.4 0.1 slice_bitcast_fusion.8
  151.5 0.4 slice.141
  152.0 14.0 %collective-permute-done.4 = f32[1,4,2,64,256]{4,3,2,1,0:T(8,128)S(1)} collective-permute-done((f32[1,4,2,64,256]{4,3,2,1,0:T(8,128)S(1)}, f32[1,4,2,64,256]{4,3,2,1,0:T(8,128)S(1)}, u32[]{:S(2)}, u32[]{:S(2)}) %collective-permute-start.4) | collective-permute-done | bytes 524320 | tf_op jit(solution)/shard_map/ppermute | solution.py:26
  166.0 1.6 fusion.14
  167.7 2.0 copy-done.1
  169.7 0.4 multiply_add_fusion.8
  170.1 48.9 %while.10 = (s32[]{:T(128)}, f32[4,2,64,256]{3,2,1,0:T(8,128)S(1)}, f32[1,2,64,256]{3,2,1,0:T(8,128)S(1)}, f32[4,2,64,256]{3,2,1,0:T(8,128)S(1)}, s32[]{:T(128)}) while((s32[]{:T(128)}, f32[4,2,64,256]{3,2,1,0:T(8,128)S(1)}, f32[1,2,64,256]{3,2,1,0:T(8,128)S(1)}, f32[4,2,64,256]{3,2,1,0:T(8,128)S(1)}, s32[]{:T(128)}) %tuple.34), condition=%wide.region_1.2_spmd, body=%wide.region_0.1_spmd.sunk | while | flops 262146 | bytes 3801189 | solution.py:79
  170.1 0.1 multiply_add_fusion.13
  170.2 1.3 collective-permute-start
  171.5 15.6 %collective-permute-done = f32[4,2,64,256]{3,2,1,0:T(8,128)S(1)} collective-permute-done((f32[4,2,64,256]{3,2,1,0:T(8,128)S(1)}, f32[4,2,64,256]{3,2,1,0:T(8,128)S(1)}, u32[]{:S(2)}, u32[]{:S(2)}) %collective-permute-start) | collective-permute-done | bytes 524320 | tf_op jit(solution)/shard_map/while/body/eval_jaxpr/ppermute | solution.py:26
  187.1 0.1 multiply_add_fusion.13
  187.2 1.3 collective-permute-start
  188.5 15.0 %collective-permute-done = f32[4,2,64,256]{3,2,1,0:T(8,128)S(1)} collective-permute-done((f32[4,2,64,256]{3,2,1,0:T(8,128)S(1)}, f32[4,2,64,256]{3,2,1,0:T(8,128)S(1)}, u32[]{:S(2)}, u32[]{:S(2)}) %collective-permute-start) | collective-permute-done | bytes 524320 | tf_op jit(solution)/shard_map/while/body/eval_jaxpr/ppermute | solution.py:26
  203.5 0.1 multiply_add_fusion.13
  203.6 1.3 collective-permute-start
  204.9 14.1 %collective-permute-done = f32[4,2,64,256]{3,2,1,0:T(8,128)S(1)} collective-permute-done((f32[4,2,64,256]{3,2,1,0:T(8,128)S(1)}, f32[4,2,64,256]{3,2,1,0:T(8,128)S(1)}, u32[]{:S(2)}, u32[]{:S(2)}) %collective-permute-start) | collective-permute-done | bytes 524320 | tf_op jit(solution)/shard_map/while/body/eval_jaxpr/ppermute | solution.py:26
  219.0 2.8 %bitcast_dynamic-update-slice_fusion.7 = (f32[8,4,2,64,256]{4,3,2,1,0:T(8,128)S(1)}, f32[4,2,64,256]{3,2,1,0:T(8,128)S(1)}, f32[4,2,64,256]{3,2,1,0:T(8,128)S(1)}, f32[4,2,64,256]{3,2,1,0:T(8,128)S(1)}) fusion(f32[8,4,2,64,256]{4,3,2,1,0:T(8,128)} %copy-done.1, f32[2,64,256]{2,1,0:T(8,128)S(1)} %get-tuple-element.52, ...), kind=kLoop, calls=%fused_computation.51 | loop fusion | flops 2097151 | bytes 7864320
  221.8 0.7 copy-done.2
  222.5 0.1 bitcast_dynamic-update-slice_fusion.6
  222.6 0.1 bitcast_dynamic-update-slice_fusion.4
  222.7 0.1 bitcast_dynamic-update-slice_fusion.2
  222.9 2.0 copy-done.6
  224.9 0.9 bitcast_dynamic-update-slice_fusion
  (23 shorter events, 0.2 us)
Async XLA Ops:
  6.5 138.0 %copy-start = (f32[64,64]{1,0:T(8,128)S(1)}, f32[64,64]{1,0:T(8,128)}, u32[]{:S(2)}) copy-start(f32[64,64]{1,0:T(8,128)} %param.15) | copy-start | bytes 49156
  6.5 102.2 %all-gather.2.cloned.1.call-start = ((), (), s32[]{:S(2)}) async-start(), calls=%async_computation | async-start | bytes 10485760 | tf_op jit(solution)/shard_map/all_gather | solution.py:47
  15.7 2.6 %copy-start.7 = (f32[8]{0:T(128)S(1)}, f32[8]{0:T(128)}, u32[]{:S(2)}) copy-start(f32[8]{0:T(128)} %param.16) | copy-start | bytes 100
  15.7 3.9 %copy-start.8 = (s32[32]{0:T(128)S(1)}, s32[32]{0:T(128)}, u32[]{:S(2)}) copy-start(s32[32]{0:T(128)} %param.12) | copy-start | bytes 388
  15.7 4.0 %copy-start.4 = (f32[2,64,256]{2,1,0:T(8,128)S(1)}, f32[2,64,256]{2,1,0:T(8,128)}, u32[]{:S(2)}) copy-start(f32[2,64,256]{2,1,0:T(8,128)} %param.17) | copy-start | bytes 393220
  18.2 101.5 %collective-permute-start.3 = (f32[1]{0:T(128)S(1)}, f32[1]{0:T(128)}, u32[]{:S(2)}, u32[]{:S(2)}) collective-permute-start(f32[1]{0:T(128)S(1)} %bitcast.140), channel_id=1, source_target_pairs={{1,0},{2,1},{3,2},{5,4},{6,5},{7,6},{9,8},{10,9},{11,10},{13,12},{... | collective-permute-start | bytes 20 | tf_op jit(solution)/shard_map/ppermute | solution.py:26
  108.7 4.8 %copy-start.3 = (f32[8,4,2,64,256]{4,3,2,1,0:T(8,128)S(1)}, f32[8,4,2,64,256]{4,3,2,1,0:T(8,128)}, u32[]{:S(2)}) copy-start(f32[8,4,2,64,256]{4,3,2,1,0:T(8,128)} %param.10) | copy-start | bytes 12582916
  115.2 4.0 %copy-start.5 = (f32[64,256]{1,0:T(8,128)S(1)}, f32[64,256]{1,0:T(8,128)}, u32[]{:S(2)}) copy-start(f32[64,256]{1,0:T(8,128)} %param.14) | copy-start | bytes 196612
  115.4 25.6 %collective-permute-start.1 = (bf16[8,4,1,64,256]{4,3,2,1,0:T(8,128)(2,1)S(1)}, bf16[8,4,1,64,256]{4,3,2,1,0:T(8,128)(2,1)S(1)}, u32[]{:S(2)}, u32[]{:S(2)}) collective-permute-start(bf16[8,4,1,64,256]{4,3,2,1,0:T(8,128)(2,1)S(1)} %get-tuple-element.42), channel_id=1, source_target_pairs={{0,4},{4,8},{8,12},{12,16},{16,20},{20,24},{24,28},{28,0},{1,5},{5... | collective-permute-start | bytes 3145736 | tf_op jit(solution)/shard_map/ppermute | solution.py:14
  115.7 25.4 %collective-permute-start.2 = (bf16[8,4,1,64,256]{4,3,2,1,0:T(8,128)(2,1)S(1)}, bf16[8,4,1,64,256]{4,3,2,1,0:T(8,128)(2,1)S(1)}, u32[]{:S(2)}, u32[]{:S(2)}) collective-permute-start(bf16[8,4,1,64,256]{4,3,2,1,0:T(8,128)(2,1)S(1)} %get-tuple-element.43), channel_id=1, source_target_pairs={{4,0},{8,4},{12,8},{16,12},{20,16},{24,20},{28,24},{0,28},{5,1},{9... | collective-permute-start | bytes 3145736 | tf_op jit(solution)/shard_map/ppermute | solution.py:16
  150.0 16.0 %collective-permute-start.4 = (f32[1,4,2,64,256]{4,3,2,1,0:T(8,128)S(1)}, f32[1,4,2,64,256]{4,3,2,1,0:T(8,128)S(1)}, u32[]{:S(2)}, u32[]{:S(2)}) collective-permute-start(f32[1,4,2,64,256]{4,3,2,1,0:T(8,128)S(1)} %slice.142), channel_id=1, source_target_pairs={{1,0},{2,1},{3,2},{5,4},{6,5},{7,6},{9,8},{10,9},{11,10},{13,12},{... | collective-permute-start | bytes 1572872 | tf_op jit(solution)/shard_map/ppermute | solution.py:26
  167.6 2.0 copy-start.1
  170.2 16.9 %collective-permute-start = (f32[4,2,64,256]{3,2,1,0:T(8,128)S(1)}, f32[4,2,64,256]{3,2,1,0:T(8,128)S(1)}, u32[]{:S(2)}, u32[]{:S(2)}) collective-permute-start(f32[4,2,64,256]{3,2,1,0:T(8,128)S(1)} %multiply_add_fusion.13), channel_id=1, source_target_pairs={{1,0},{2,1},{3,2},{5,4},{6,5},{7,6},{9,8},{10,9},{11,10},{13,12},{... | collective-permute-start | bytes 1572872 | tf_op jit(solution)/shard_map/while/body/eval_jaxpr/ppermute | solution.py:26
  187.2 16.3 %collective-permute-start = (f32[4,2,64,256]{3,2,1,0:T(8,128)S(1)}, f32[4,2,64,256]{3,2,1,0:T(8,128)S(1)}, u32[]{:S(2)}, u32[]{:S(2)}) collective-permute-start(f32[4,2,64,256]{3,2,1,0:T(8,128)S(1)} %multiply_add_fusion.13), channel_id=1, source_target_pairs={{1,0},{2,1},{3,2},{5,4},{6,5},{7,6},{9,8},{10,9},{11,10},{13,12},{... | collective-permute-start | bytes 1572872 | tf_op jit(solution)/shard_map/while/body/eval_jaxpr/ppermute | solution.py:26
  203.6 15.4 %collective-permute-start = (f32[4,2,64,256]{3,2,1,0:T(8,128)S(1)}, f32[4,2,64,256]{3,2,1,0:T(8,128)S(1)}, u32[]{:S(2)}, u32[]{:S(2)}) collective-permute-start(f32[4,2,64,256]{3,2,1,0:T(8,128)S(1)} %multiply_add_fusion.13), channel_id=1, source_target_pairs={{1,0},{2,1},{3,2},{5,4},{6,5},{7,6},{9,8},{10,9},{11,10},{13,12},{... | collective-permute-start | bytes 1572872 | tf_op jit(solution)/shard_map/while/body/eval_jaxpr/ppermute | solution.py:26
  219.0 3.4 %copy-start.2 = (f32[8,4,2,64,256]{4,3,2,1,0:T(8,128)S(1)}, f32[8,4,2,64,256]{4,3,2,1,0:T(8,128)}, u32[]{:S(2)}) copy-start(f32[8,4,2,64,256]{4,3,2,1,0:T(8,128)} %copy-done.1) | copy-start | bytes 12582916
  222.9 2.0 copy-start.6
Sparse Core Ops, SparseCore 0:
  18.4 90.2 all-gather.1
where the time goes:
time: 233 us
  waiting for transfers between devices  168 us (72%)
  matrix products  18.9 us (8%)
  between operations  13.7 us (6%)
  other arithmetic  12.9 us (6%)
  starting transfers between devices  10.2 us (4%)
  local copies, waits for them, and re-layouts  8.76 us (4%)
    all_gather x1, waiting for transfers between devices, one_step(): lax.all_gather(flat_parents, 'mom', axis=0, tiled=True)  88.9 us
    ppermute x5, waiting for transfers between devices, passed_along(): return lax.ppermute(block, axis, route)  58.8 us
    ppermute x1, waiting for transfers between devices, padded_2(): lax.ppermute(tail, axis, [(i, (i + 1) % count) for i in range(count)])  20.4 us
    dot_general x1, matrix products, one_step(): jnp.einsum('st,qtxzr->qsxzr', onehot, state, precision=lax.Precision.HIGH...  8.71 us
    unnamed x22, local copies, waits for them, and re-layouts  7.36 us
    ppermute x5, starting transfers between devices, passed_along(): return lax.ppermute(block, axis, route)  6.46 us
    dot_general x1, matrix products, one_step(): jnp.einsum('yz,psxzr->psxyr', height_inverse, halfway, precision=lax.Prec...  5.41 us
    dot_general x1, matrix products, one_step(): jnp.dot(kernel_rows, lax.all_gather(flat_parents, 'mom', axis=0, tiled=Tr...  4.81 us
  transfers between devices with their start and end apart: 8, of which 6 were waited for; matrix products, arithmetic and copies ran while one was open for 4% of the time, Pallas kernels for 0%

commit v1 on v0

--- a/solution.py
+++ b/solution.py
@@ -2,6 +2,28 @@
 import jax.numpy as jnp
 from jax import lax
 from jax.sharding import PartitionSpec as P
+
+
+def joined_along(pieces, dim):
+    pieces = jnp.moveaxis(pieces, 0, dim)
+    lengths = pieces.shape
+    return pieces.reshape(*lengths[:dim], lengths[dim] * lengths[dim + 1], *lengths[dim + 2 :])
+
+
+def gather_around(x, axis, dim):
+    size = lax.axis_size(axis)
+    pairs = [(i, (i + 1) % size) for i in range(size)]
+    back = [(b, a) for a, b in pairs]
+    lower, upper = ([], [])
+    for step in range(size - 1):
+        if step % 2 == 0:
+            lower.append(lax.ppermute(lower[-1] if lower else x, axis, pairs))
+        else:
+            upper.append(lax.ppermute(upper[-1] if upper else x, axis, back))
+    parts = jnp.stack([*lower[::-1], x, *upper])
+    shift = lax.axis_index(axis) - len(lower)
+    parts = parts[(jnp.arange(size) - shift) % size]
+    return joined_along(parts, dim)
 
 
 def padded_2(cells, sides, width):
@@ -43,9 +65,7 @@
     flat_parents = parents.reshape(bins_here, -1)
     kernel_rows = lax.dynamic_slice_in_dim(kernel, first_bin, bins_here, 0)
     source = jnp.dot(
-        kernel_rows,
-        lax.all_gather(flat_parents, "mom", axis=0, tiled=True),
-        preferred_element_type=jnp.float32,
+        kernel_rows, gather_around(flat_parents, "mom", 0), preferred_element_type=jnp.float32
     )
     sourced = state + source.reshape(state.shape)
     padded = padded_2(sourced.astype(jnp.bfloat16), (("phi", 2),), 1).astype(sourced.dtype)

time: 233 us -> 306 us (1.31)
  waiting for transfers between devices: 168 us -> 209 us
  local copies, waits for them, and re-layouts: 8.76 us -> 33.3 us
  between operations: 13.7 us -> 0.33 us
  other arithmetic: 12.9 us -> 23.6 us
  matrix products: 18.9 us -> 24.1 us
  starting transfers between devices: 10.2 us -> 15.2 us
    ppermute x0 -> x3, waiting for transfers between devices: none -> 131 us  [the longest x2 90.3 us: gather_around(): lower.append(lax.ppermute(lower[-1] if lower else x, axis, pairs))]
    all_gather x1 -> x0, waiting for transfers between devices: 88.9 us -> none  [one_step(): lax.all_gather(flat_parents, 'mom', axis=0, tiled=True)]
    gather x0 -> x3, local copies, waits for them, and re-layouts: none -> 13.6 us  [gather_around(): parts = parts[(jnp.arange(size) - shift) % size]]
    unnamed x22 -> x23, local copies, waits for them, and re-layouts: 7.36 us -> 16.1 us
    unnamed x4 -> x5, other arithmetic: 2.99 us -> 10.3 us
    ppermute x0 -> x3, starting transfers between devices: none -> 5 us  [the longest x2 4.04 us: gather_around(): lower.append(lax.ppermute(lower[-1] if lower else x, axis, pairs))]
    dot_general x1, matrix products: 4.81 us -> 9.77 us  [one_step(): jnp.dot(kernel_rows, gather_around(flat_parents, 'mom', 0), preferred_ele...]
    another operation x0 -> x1, other arithmetic: none -> 4.34 us  [gather_around(): parts = jnp.stack([*lower[::-1], x, *upper])]
  transfers between devices with their start and end apart: 8 -> 10, of which waited for: 6 -> 8; matrix products, arithmetic and copies ran while one was open for 4% -> 16% of each run, Pallas kernels for 0% -> 0%
where the time goes in v1:
time: 306 us
  waiting for transfers between devices  209 us (68%)
  local copies, waits for them, and re-layouts  33.3 us (11%)
  matrix products  24.1 us (8%)
  other arithmetic  23.6 us (8%)
  starting transfers between devices  15.2 us (5%)
    ppermute x2, waiting for transfers between devices, gather_around(): lower.append(lax.ppermute(lower[-1] if lower else x, axis, pairs))  90.3 us
    ppermute x5, waiting for transfers between devices, passed_along(): return lax.ppermute(block, axis, route)  58.9 us
    ppermute x1, waiting for transfers between devices, gather_around(): upper.append(lax.ppermute(upper[-1] if upper else x, axis, back))  40.3 us
    ppermute x1, waiting for transfers between devices, padded_2(): lax.ppermute(tail, axis, [(i, (i + 1) % count) for i in range(count)])  19.9 us
    unnamed x23, local copies, waits for them, and re-layouts  16.1 us
    gather x3, local copies, waits for them, and re-layouts, gather_around(): parts = parts[(jnp.arange(size) - shift) % size]  13.6 us
    unnamed x5, other arithmetic  10.3 us
    dot_general x1, matrix products, one_step(): jnp.dot(kernel_rows, gather_around(flat_parents, 'mom', 0), preferred_ele...  9.77 us
  transfers between devices with their start and end apart: 10, of which 8 were waited for; matrix products, arithmetic and copies ran while one was open for 16% of the time, Pallas kernels for 0%

profile of v1, /device:TPU:0, one launch (start us, length us, event | category | flops | bytes accessed | tf_op | source)
XLA Modules:
  0.0 305.9 jit_solution(7864482328595004846)
XLA Ops:
  0.0 8.7 %convert_bitcast_fusion = bf16[8,4,2,64,256]{4,1,3,2,0:T(4,128)(2,1)S(1)} fusion(f32[8,4,2,64,256]{4,3,2,1,0:T(8,128)} %param.10, s32[4]{0:T(128)} %param.13), kind=kOutput, calls=%fused_computation.28 | convolution fusion | flops 51380240 | bytes 6291472 | tf_op jit(solution)/shard_map/st,qtxzr->qsxzr/dot_general | solution.py:59
  8.7 0.4 copy.13
  9.2 2.5 copy.21
  11.7 2.9 collective-permute-start.1
  14.6 1.0 collective-permute-start.3
  15.6 46.8 %collective-permute-done.1 = bf16[8,131072]{1,0:T(8,128)(2,1)} collective-permute-done((bf16[8,131072]{1,0:T(8,128)(2,1)}, bf16[8,131072]{1,0:T(8,128)(2,1)}, u32[]{:S(2)}, u32[]{:S(2)}) %collective-permute-start.1) | collective-permute-done | bytes 2097184 | tf_op jit(solution)/shard_map/ppermute | solution.py:20
  62.3 1.1 collective-permute-start.2
  63.4 1.5 collective-permute-start.6
  64.9 2.3 stack_reshape.3
  67.3 0.2 broadcast_multiply_fusion
  67.5 40.3 %collective-permute-done.3 = bf16[8,131072]{1,0:T(8,128)(2,1)} collective-permute-done((bf16[8,131072]{1,0:T(8,128)(2,1)}, bf16[8,131072]{1,0:T(8,128)(2,1)}, u32[]{:S(2)}, u32[]{:S(2)}) %collective-permute-start.3) | collective-permute-done | bytes 2097184 | tf_op jit(solution)/shard_map/ppermute | solution.py:22
  107.8 43.5 %collective-permute-done.2 = bf16[8,131072]{1,0:T(8,128)(2,1)} collective-permute-done((bf16[8,131072]{1,0:T(8,128)(2,1)}, bf16[8,131072]{1,0:T(8,128)(2,1)}, u32[]{:S(2)}, u32[]{:S(2)}) %collective-permute-start.2) | collective-permute-done | bytes 2097184 | tf_op jit(solution)/shard_map/ppermute | solution.py:20
  151.4 4.3 %pad_maximum_fusion = bf16[4,8,131072]{2,1,0:T(8,128)(2,1)S(1)} fusion(bf16[1,8,131072]{2,1,0:T(8,128)(2,1)} %bitcast.8, bf16[1,8,131072]{2,1,0:T(8,128)(2,1)} %stack_reshape.3, bf16[1,8,131072]{2,1,0:T(8,128)(2,1)} %bitcast.7, bf16[1,8,131072]{2,1,0:T(8,128)(2,1)} %bitcast.6), kind=kLoop, calls=%fused_computation.3 | loop fusion | flops 12582912 | bytes 16777216 | tf_op jit(solution)/shard_map/stack | solution.py:23
  155.7 3.6 %fusion.39 = (bf16[4,8,65536]{2,1,0:T(8,128)(2,1)}, bf16[4,8,65536]{2,1,0:T(8,128)(2,1)}) fusion(bf16[4,8,131072]{2,1,0:T(8,128)(2,1)S(1)} %pad_maximum_fusion), kind=kLoop, calls=%fused_computation.93 | loop fusion | bytes 16777216 | tf_op jit(solution)/shard_map/gather | solution.py:25
  159.3 5.0 %gather_fusion = bf16[4,8,65536]{2,1,0:T(8,128)(2,1)} fusion(bf16[4,8,65536]{2,1,0:T(8,128)(2,1)} %get-tuple-element.40, s32[1024]{0:T(1024)S(1)} %pad_clamp_fusion), kind=kCustom, calls=%fused_computation | custom fusion | bytes 8388624 | tf_op jit(solution)/shard_map/gather | solution.py:25
  164.3 5.0 %gather_fusion.1 = bf16[4,8,65536]{2,1,0:T(8,128)(2,1)} fusion(bf16[4,8,65536]{2,1,0:T(8,128)(2,1)} %get-tuple-element.41, s32[1024]{0:T(1024)S(1)} %pad_clamp_fusion), kind=kCustom, calls=%fused_computation.1 | custom fusion | bytes 8388624 | tf_op jit(solution)/shard_map/gather | solution.py:25
  169.3 7.3 %pad_maximum_fusion.1 = bf16[4,8,131072]{2,1,0:T(8,128)(2,1)} fusion(bf16[4,8,65536]{2,1,0:T(8,128)(2,1)} %gather_fusion.1, bf16[4,8,65536]{2,1,0:T(8,128)(2,1)} %gather_fusion), kind=kLoop, calls=%fused_computation.4 | loop fusion | flops 16777216 | bytes 16777216
  176.6 8.8 %copy.22 = bf16[4,8,512,256]{3,2,1,0:T(8,128)(2,1)} copy(bf16[4,8,512,256]{3,1,2,0:T(8,128)(2,1)} %bitcast.157) | data formatting | bytes 16777216
  185.4 9.8 %fusion.42 = (bf16[8,4,2,64,256]{4,0,3,2,1:T(8,128)(2,1)S(1)}, f32[8,4,2,64,256]{4,0,3,2,1:T(8,128)S(1)}) fusion(bf16[4,2,64,256,32]{3,2,1,0,4:T(8,128)(2,1)} %bitcast.156, bf16[32,32]{1,0:T(8,128)(2,1)} %param.11, s32[]{:T(128)S(6)} %select_n.32, s32[32]{0:T(128)S(1)} %copy-done.8, s32[8]{0:T(128)S(1)} %dynamic-slice, f32[8,4,2,64,256]{4,3,2,1,0:T(8,128)S(1)} %copy-done.3), kind=kOutput, calls=%fused_computation.96 | convolution fusion | flops 69206528 | bytes 18876580 | tf_op jit(solution)/shard_map/dot_general | solution.py:67
  195.2 0.1 fusion.40
  195.4 3.5 %collective-permute-start.5 = (bf16[8,4,1,64,256]{4,0,3,2,1:T(8,128)(2,1)S(1)}, bf16[8,4,1,64,256]{4,0,3,2,1:T(8,128)(2,1)S(1)}, u32[]{:S(2)}, u32[]{:S(2)}) collective-permute-start(bf16[8,4,1,64,256]{4,0,3,2,1:T(8,128)(2,1)S(1)} %get-tuple-element.43), channel_id=1, source_target_pairs={{4,0},{8,4},{12,8},{16,12},{20,16},{24,20},{28,24},{0,28},{5,1},{9... | collective-permute-start | bytes 3145736 | tf_op jit(solution)/shard_map/ppermute | solution.py:38
  198.9 0.1 fusion.41
  199.1 0.3 fusion.24
  199.4 0.7 multiply_bitcast_fusion.1
  200.1 0.3 fusion.22
  200.4 19.9 %collective-permute-done.4 = bf16[8,4,1,64,256]{4,0,3,2,1:T(8,128)(2,1)S(1)} collective-permute-done((bf16[8,4,1,64,256]{4,0,3,2,1:T(8,128)(2,1)S(1)}, bf16[8,4,1,64,256]{4,0,3,2,1:T(8,128)(2,1)S(1)}, u32[]{:S(2)}, u32[]{:S(2)}) %collective-permute-start.4) | collective-permute-done | bytes 1048608 | tf_op jit(solution)/shard_map/ppermute | solution.py:36
  220.3 0.7 maximum_convert_fusion
  220.9 2.7 fusion.5
  223.6 0.7 multiply_add_fusion.1
  224.3 5.6 %fusion.15 = f32[8,4,2,64,256]{4,3,2,1,0:T(8,128)S(1)} fusion(f32[8,4,2,64,256]{4,0,3,2,1:T(8,128)S(1)} %multiply_add_fusion.1, f32[64,64]{1,0:T(8,128)S(1)} %copy-done), kind=kOutput, calls=%fused_computation.27 | convolution fusion | flops 805306368 | bytes 8404992 | tf_op jit(solution)/shard_map/yz,psxzr->psxyr/dot_general | solution.py:78
  230.0 1.3 collective-permute-start.7
  231.4 0.1 slice_bitcast_fusion.8
  231.5 0.4 slice.145
  231.9 13.5 %collective-permute-done.7 = f32[1,4,2,64,256]{4,3,2,1,0:T(8,128)S(1)} collective-permute-done((f32[1,4,2,64,256]{4,3,2,1,0:T(8,128)S(1)}, f32[1,4,2,64,256]{4,3,2,1,0:T(8,128)S(1)}, u32[]{:S(2)}, u32[]{:S(2)}) %collective-permute-start.7) | collective-permute-done | bytes 524320 | tf_op jit(solution)/shard_map/ppermute | solution.py:48
  245.4 1.7 fusion.10
  247.2 2.0 copy-done.1
  249.2 0.4 multiply_add_fusion.9
  249.6 49.5 %while.10 = (s32[]{:T(128)}, f32[4,2,64,256]{3,2,1,0:T(8,128)S(1)}, f32[1,2,64,256]{3,2,1,0:T(8,128)S(1)}, f32[4,2,64,256]{3,2,1,0:T(8,128)S(1)}, s32[]{:T(128)}) while((s32[]{:T(128)}, f32[4,2,64,256]{3,2,1,0:T(8,128)S(1)}, f32[1,2,64,256]{3,2,1,0:T(8,128)S(1)}, f32[4,2,64,256]{3,2,1,0:T(8,128)S(1)}, s32[]{:T(128)}) %tuple.35), condition=%wide.region_1.2_spmd, body=%wide.region_0.1_spmd.sunk | while | flops 262146 | bytes 3801189 | solution.py:99
  249.7 1.3 collective-permute-start
  251.0 15.3 %collective-permute-done = f32[4,2,64,256]{3,2,1,0:T(8,128)S(1)} collective-permute-done((f32[4,2,64,256]{3,2,1,0:T(8,128)S(1)}, f32[4,2,64,256]{3,2,1,0:T(8,128)S(1)}, u32[]{:S(2)}, u32[]{:S(2)}) %collective-permute-start) | collective-permute-done | bytes 524320 | tf_op jit(solution)/shard_map/while/body/eval_jaxpr/ppermute | solution.py:48
  266.5 1.3 collective-permute-start
  267.8 15.6 %collective-permute-done = f32[4,2,64,256]{3,2,1,0:T(8,128)S(1)} collective-permute-done((f32[4,2,64,256]{3,2,1,0:T(8,128)S(1)}, f32[4,2,64,256]{3,2,1,0:T(8,128)S(1)}, u32[]{:S(2)}, u32[]{:S(2)}) %collective-permute-start) | collective-permute-done | bytes 524320 | tf_op jit(solution)/shard_map/while/body/eval_jaxpr/ppermute | solution.py:48
  283.4 1.3 collective-permute-start
  284.7 14.4 %collective-permute-done = f32[4,2,64,256]{3,2,1,0:T(8,128)S(1)} collective-permute-done((f32[4,2,64,256]{3,2,1,0:T(8,128)S(1)}, f32[4,2,64,256]{3,2,1,0:T(8,128)S(1)}, u32[]{:S(2)}, u32[]{:S(2)}) %collective-permute-start) | collective-permute-done | bytes 524320 | tf_op jit(solution)/shard_map/while/body/eval_jaxpr/ppermute | solution.py:48
  299.2 2.8 bitcast_dynamic-update-slice_fusion.7
  302.0 0.7 copy-done.2
  303.0 2.0 copy-done.6
  305.1 0.9 bitcast_dynamic-update-slice_fusion
  (35 shorter events, 1.0 us)
Async XLA Ops:
  0.0 224.3 %copy-start = (f32[64,64]{1,0:T(8,128)S(1)}, f32[64,64]{1,0:T(8,128)}, u32[]{:S(2)}) copy-start(f32[64,64]{1,0:T(8,128)} %param.15) | copy-start | bytes 49156
  8.7 54.7 %copy-start.7 = (f32[8]{0:T(128)S(1)}, f32[8]{0:T(128)}, u32[]{:S(2)}) copy-start(f32[8]{0:T(128)} %param.16) | copy-start | bytes 100
  9.1 58.1 %copy-start.8 = (s32[32]{0:T(128)S(1)}, s32[32]{0:T(128)}, u32[]{:S(2)}) copy-start(s32[32]{0:T(128)} %param.12) | copy-start | bytes 388
  9.1 58.2 %copy-start.4 = (f32[2,64,256]{2,1,0:T(8,128)S(1)}, f32[2,64,256]{2,1,0:T(8,128)}, u32[]{:S(2)}) copy-start(f32[2,64,256]{2,1,0:T(8,128)} %param.17) | copy-start | bytes 393220
  11.7 50.7 %collective-permute-start.1 = (bf16[8,131072]{1,0:T(8,128)(2,1)}, bf16[8,131072]{1,0:T(8,128)(2,1)}, u32[]{:S(2)}, u32[]{:S(2)}) collective-permute-start(bf16[8,131072]{1,0:T(8,128)(2,1)} %bitcast.50), channel_id=1, source_target_pairs={{0,1},{1,2},{2,3},{3,0},{4,5},{5,6},{6,7},{7,4},{8,9},{9,10},{10,1... | collective-permute-start | bytes 6291464 | tf_op jit(solution)/shard_map/ppermute | solution.py:20
  14.6 93.2 %collective-permute-start.3 = (bf16[8,131072]{1,0:T(8,128)(2,1)}, bf16[8,131072]{1,0:T(8,128)(2,1)}, u32[]{:S(2)}, u32[]{:S(2)}) collective-permute-start(bf16[8,131072]{1,0:T(8,128)(2,1)} %bitcast.50), channel_id=1, source_target_pairs={{1,0},{2,1},{3,2},{0,3},{5,4},{6,5},{7,6},{4,7},{9,8},{10,9},{11,1... | collective-permute-start | bytes 6291464 | tf_op jit(solution)/shard_map/ppermute | solution.py:22
  62.3 89.1 %collective-permute-start.2 = (bf16[8,131072]{1,0:T(8,128)(2,1)}, bf16[8,131072]{1,0:T(8,128)(2,1)}, u32[]{:S(2)}, u32[]{:S(2)}) collective-permute-start(bf16[8,131072]{1,0:T(8,128)(2,1)} %collective-permute-done.1), channel_id=1, source_target_pairs={{0,1},{1,2},{2,3},{3,0},{4,5},{5,6},{6,7},{7,4},{8,9},{9,10},{10,1... | collective-permute-start | bytes 6291464 | tf_op jit(solution)/shard_map/ppermute | solution.py:20
  63.4 135.9 %collective-permute-start.6 = (f32[1]{0:T(128)S(1)}, f32[1]{0:T(128)}, u32[]{:S(2)}, u32[]{:S(2)}) collective-permute-start(f32[1]{0:T(128)S(1)} %bitcast.160), channel_id=1, source_target_pairs={{1,0},{2,1},{3,2},{5,4},{6,5},{7,6},{9,8},{10,9},{11,10},{13,12},{... | collective-permute-start | bytes 20 | tf_op jit(solution)/shard_map/ppermute | solution.py:48
  176.6 8.8 %copy-start.3 = (f32[8,4,2,64,256]{4,3,2,1,0:T(8,128)S(1)}, f32[8,4,2,64,256]{4,3,2,1,0:T(8,128)}, u32[]{:S(2)}) copy-start(f32[8,4,2,64,256]{4,3,2,1,0:T(8,128)} %param.10) | copy-start | bytes 12582916
  195.2 3.8 %copy-start.5 = (f32[64,256]{1,0:T(8,128)S(1)}, f32[64,256]{1,0:T(8,128)}, u32[]{:S(2)}) copy-start(f32[64,256]{1,0:T(8,128)} %param.14) | copy-start | bytes 196612
  195.3 24.9 %collective-permute-start.4 = (bf16[8,4,1,64,256]{4,0,3,2,1:T(8,128)(2,1)S(1)}, bf16[8,4,1,64,256]{4,0,3,2,1:T(8,128)(2,1)S(1)}, u32[]{:S(2)}, u32[]{:S(2)}) collective-permute-start(bf16[8,4,1,64,256]{4,0,3,2,1:T(8,128)(2,1)S(1)} %get-tuple-element.42), channel_id=1, source_target_pairs={{0,4},{4,8},{8,12},{12,16},{16,20},{20,24},{24,28},{28,0},{1,5},{5... | collective-permute-start | bytes 3145736 | tf_op jit(solution)/shard_map/ppermute | solution.py:36
  195.4 24.9 %collective-permute-start.5 = (bf16[8,4,1,64,256]{4,0,3,2,1:T(8,128)(2,1)S(1)}, bf16[8,4,1,64,256]{4,0,3,2,1:T(8,128)(2,1)S(1)}, u32[]{:S(2)}, u32[]{:S(2)}) collective-permute-start(bf16[8,4,1,64,256]{4,0,3,2,1:T(8,128)(2,1)S(1)} %get-tuple-element.43), channel_id=1, source_target_pairs={{4,0},{8,4},{12,8},{16,12},{20,16},{24,20},{28,24},{0,28},{5,1},{9... | collective-permute-start | bytes 3145736 | tf_op jit(solution)/shard_map/ppermute | solution.py:38
  230.0 15.4 %collective-permute-start.7 = (f32[1,4,2,64,256]{4,3,2,1,0:T(8,128)S(1)}, f32[1,4,2,64,256]{4,3,2,1,0:T(8,128)S(1)}, u32[]{:S(2)}, u32[]{:S(2)}) collective-permute-start(f32[1,4,2,64,256]{4,3,2,1,0:T(8,128)S(1)} %slice.146), channel_id=1, source_target_pairs={{1,0},{2,1},{3,2},{5,4},{6,5},{7,6},{9,8},{10,9},{11,10},{13,12},{... | collective-permute-start | bytes 1572872 | tf_op jit(solution)/shard_map/ppermute | solution.py:48
  247.2 2.0 copy-start.1
  249.7 16.6 %collective-permute-start = (f32[4,2,64,256]{3,2,1,0:T(8,128)S(1)}, f32[4,2,64,256]{3,2,1,0:T(8,128)S(1)}, u32[]{:S(2)}, u32[]{:S(2)}) collective-permute-start(f32[4,2,64,256]{3,2,1,0:T(8,128)S(1)} %multiply_add_fusion.14), channel_id=1, source_target_pairs={{1,0},{2,1},{3,2},{5,4},{6,5},{7,6},{9,8},{10,9},{11,10},{13,12},{... | collective-permute-start | bytes 1572872 | tf_op jit(solution)/shard_map/while/body/eval_jaxpr/ppermute | solution.py:48
  266.5 16.9 %collective-permute-start = (f32[4,2,64,256]{3,2,1,0:T(8,128)S(1)}, f32[4,2,64,256]{3,2,1,0:T(8,128)S(1)}, u32[]{:S(2)}, u32[]{:S(2)}) collective-permute-start(f32[4,2,64,256]{3,2,1,0:T(8,128)S(1)} %multiply_add_fusion.14), channel_id=1, source_target_pairs={{1,0},{2,1},{3,2},{5,4},{6,5},{7,6},{9,8},{10,9},{11,10},{13,12},{... | collective-permute-start | bytes 1572872 | tf_op jit(solution)/shard_map/while/body/eval_jaxpr/ppermute | solution.py:48
  283.4 15.7 %collective-permute-start = (f32[4,2,64,256]{3,2,1,0:T(8,128)S(1)}, f32[4,2,64,256]{3,2,1,0:T(8,128)S(1)}, u32[]{:S(2)}, u32[]{:S(2)}) collective-permute-start(f32[4,2,64,256]{3,2,1,0:T(8,128)S(1)} %multiply_add_fusion.14), channel_id=1, source_target_pairs={{1,0},{2,1},{3,2},{5,4},{6,5},{7,6},{9,8},{10,9},{11,10},{13,12},{... | collective-permute-start | bytes 1572872 | tf_op jit(solution)/shard_map/while/body/eval_jaxpr/ppermute | solution.py:48
  299.2 3.4 %copy-start.2 = (f32[8,4,2,64,256]{4,3,2,1,0:T(8,128)S(1)}, f32[8,4,2,64,256]{4,3,2,1,0:T(8,128)}, u32[]{:S(2)}) copy-start(f32[8,4,2,64,256]{4,3,2,1,0:T(8,128)} %copy-done.1) | copy-start | bytes 12582916
  303.0 2.0 copy-start.6
